TPU v7x, 256 devices: a whole 4x4x8 slice. The times are simulated.
256 devices in a mesh: fsdp: 64 (over z, y, core), tensor: 4 (over x).
Axes of the slice: x: 4, y: 4, z: 8, core: 2. Of those that a mesh axis runs over, the one named last changes fastest.
Arguments:
- momentum: bfloat16 [16384, 26624], P('fsdp', 'tensor'), may hold values from -6 to 6
- q_basis: float32 [256, 26624], P('fsdp', 'tensor'), may hold values from -0.0390625 to 0.0390625
Outputs:
- new_momentum: bfloat16 [16384, 26624], P('fsdp', 'tensor')
- update: bfloat16 [16384, 26624], P('fsdp', 'tensor')
- q_next: float32 [256, 26624], P('fsdp', 'tensor')
All inputs are finite; a program needn't handle non-finite values.
Results may differ from a plain program's by a relative error of at most 0.0073.
Values may be sent and summed in bfloat16 or wider, within the bound.
No kernel may reach another device: no remote copies, remote signals or barrier semaphores. Data moves between devices by JAX's collectives and lax.ppermute only.
A program may use at most 64 MiB of HBM per device.

v0:
```python
import math

import jax
import jax.numpy as jnp
from jax import lax
from jax.sharding import PartitionSpec as P

momentum_decay = 0.95


def gram_of(matrix):
    return jnp.dot(
        matrix.T, matrix, preferred_element_type=jnp.float32, precision=lax.Precision.HIGHEST
    )


def factor_of(gram_matrix):
    width = gram_matrix.shape[0]
    ridge = 0.001 * jnp.trace(gram_matrix) / width
    return jnp.linalg.cholesky(gram_matrix + ridge * jnp.eye(width, dtype=jnp.float32))


def orthonormalize(factor, matrix):
    solved = lax.linalg.triangular_solve(
        factor, matrix, left_side=False, lower=True, transpose_a=True
    )
    return solved.astype(jnp.bfloat16)


def per_device(momentum, q_basis):
    shard_rank = q_basis.shape[0]
    rank_total = shard_rank * lax.axis_size("fsdp")
    rows_local = momentum.shape[0]
    cols_local = momentum.shape[1]
    basis_half = q_basis.astype(jnp.bfloat16)
    basis_whole = lax.all_gather(basis_half, "fsdp", axis=0, tiled=True)
    partial_proj = lax.dot_general(
        momentum, basis_whole, (((1,), (1,)), ((), ())), preferred_element_type=jnp.float32
    )
    projected = lax.psum(partial_proj, "tensor")
    gram_matrix = lax.psum(gram_of(projected), "fsdp")
    orthonormal = orthonormalize(factor_of(gram_matrix), projected)
    right_local = lax.dot_general(
        orthonormal, momentum, (((0,), (0,)), ((), ())), preferred_element_type=jnp.float32
    )
    right_factor = lax.psum(right_local, "fsdp")
    squares = lax.psum(jnp.sum(right_factor * right_factor, axis=1), "tensor")
    q_whole = right_factor / jnp.sqrt(squares + 1e-06)[:, None]
    removed = jnp.dot(
        orthonormal, right_factor.astype(jnp.bfloat16), preferred_element_type=jnp.float32
    )
    direction = jnp.dot(
        orthonormal, q_whole.astype(jnp.bfloat16), preferred_element_type=jnp.float32
    )
    position = lax.axis_index("fsdp")
    q_next = lax.dynamic_slice_in_dim(q_whole, position * shard_rank, shard_rank, 0)
    total_rows = rows_local * lax.axis_size("fsdp")
    total_cols = cols_local * lax.axis_size("tensor")
    scaling = math.sqrt(total_rows * total_cols / rank_total)
    new_momentum = (momentum.astype(jnp.float32) - (1.0 - momentum_decay) * removed).astype(
        jnp.bfloat16
    )
    update = (direction * scaling).astype(jnp.bfloat16)
    return (new_momentum, update, q_next)


def solution(mesh):
    return jax.shard_map(
        per_device,
        mesh=mesh,
        in_specs=(P("fsdp", "tensor"), P("fsdp", "tensor")),
        out_specs=(P("fsdp", "tensor"), P("fsdp", "tensor"), P("fsdp", "tensor")),
        check_vma=False,
    )
```

profile of v0, /device:TPU:1, one launch (start us, length us, event | category | flops | bytes accessed | tf_op | source)
XLA Modules:
  0.0 647.3 jit_solution(14005602605654319578)
XLA Ops:
  7.2 1.7 convert_bitcast_fusion
  9.0 85.0 %all-gather.3.cloned.1.call-done = bf16[64,4,6656]{2,1,0:T(4,128)(2,1)} async-done(((bf16[1,4,6656]{2,1,0:T(4,128)(2,1)}), bf16[64,4,6656]{2,1,0:T(4,128)(2,1)}) %all-gather.3.cloned.1.call-update) | async-done | bytes 3407888 | tf_op jit(solution)/shard_map/all_gather | solution.py:36
  94.0 6.5 %reshape.44 = bf16[256,6656]{1,0:T(8,128)(2,1)} reshape(bf16[64,4,6656]{2,1,0:T(4,128)(2,1)} %all-gather.3.cloned.1.call-done) | data formatting | bytes 6815744
  100.5 3.7 fusion.18
  104.3 41.7 %all-reduce.5.cloned.1.call-done = f32[256,256]{1,0:T(8,128)} async-done(((f32[256,256]{1,0:T(8,128)}), f32[256,256]{1,0:T(8,128)}) %all-reduce.5.cloned.1.call-update) | async-done | bytes 262160 | tf_op jit(solution)/shard_map/psum | solution.py:40
  146.1 2.3 fusion.19
  148.5 180.0 %all-reduce.7.cloned.1.call-done = f32[256,256]{0,1:T(8,128)} async-done(((f32[256,256]{0,1:T(8,128)}), f32[256,256]{0,1:T(8,128)}) %all-reduce.7.cloned.1.call-update) | async-done | bytes 262160 | tf_op jit(solution)/shard_map/psum | solution.py:41
  328.5 1.6 select_reduce_fusion
  330.7 1.7 select_add_fusion
  332.4 1.8 copy.12
  334.2 1.1 fusion.5
  335.3 0.7 copy-done.2
  336.0 11.7 %cholesky.49 = f32[128,128]{1,0:T(8,128)S(1)} custom-call(f32[128,128]{1,0:T(8,128)S(1)} %cholesky.115), custom_call_target="Cholesky" | custom-call | tf_op jit(solution)/shard_map/jit(cholesky)/cholesky | solution.py:20
  347.7 0.1 copy.13
  347.8 0.7 select_reduce_fusion.2
  348.4 11.3 %custom-call.14 = f32[1,128,128]{1,2,0:T(8,128)} custom-call(f32[1,128,128]{2,1,0:T(8,128)} %get-tuple-element.30), custom_call_target="InvertDiagBlocksLowerTriangular" | custom-call | tf_op jit(solution)/shard_map/jit(cholesky)/cholesky | solution.py:20
  359.7 1.1 fusion.9
  360.8 0.7 copy.14
  361.5 1.7 convolution_subtract_fusion.1
  363.3 13.2 %cholesky.103 = f32[128,128]{1,0:T(8,128)} custom-call(f32[128,128]{1,0:T(8,128)} %convolution_subtract_fusion.1), custom_call_target="Cholesky" | custom-call | tf_op jit(solution)/shard_map/jit(cholesky)/cholesky | solution.py:20
  376.4 0.9 copy.15
  377.4 0.9 select_reduce_fusion.1
  378.3 0.7 cholesky.111
  379.0 1.5 constant_dynamic-update-slice_fusion
  380.5 0.6 constant_dynamic-update-slice_fusion.1
  381.1 0.6 compare_reduce_fusion
  383.0 1.7 select_select_fusion
  384.8 7.2 %while.1 = (s32[]{:T(128)}, f32[256,256]{0,1:T(8,128)}, s32[2,2]{1,0:T(2,128)S(1)}, f32[2,128,128]{2,1,0:T(8,128)}, s32[]{:T(128)}) while((s32[]{:T(128)}, f32[256,256]{0,1:T(8,128)}, s32[2,2]{1,0:T(2,128)S(1)}, f32[2,128,128]{2,1,0:T(8,128)}, s32[]{:T(128)}) %tuple.28), condition=%wide.while_cond, body=%wide.while_body.sunk | while | flops 2 | bytes 393329 | solution.py:24
  384.8 0.6 fusion.30
  385.4 2.3 dynamic-slice.7
  387.7 0.1 copy.20
  387.8 0.6 bitcast_dynamic-update-slice_fusion.2
  388.4 0.6 fusion.30
  389.0 2.2 dynamic-slice.7
  391.2 0.1 copy.20
  391.3 0.6 bitcast_dynamic-update-slice_fusion.2
  391.9 21.1 %custom-call.15 = f32[2,128,128]{1,2,0:T(8,128)} custom-call(f32[2,128,128]{2,1,0:T(8,128)} %get-tuple-element.10), custom_call_target="InvertDiagBlocksLowerTriangular" | custom-call | tf_op jit(solution)/shard_map/triangular_solve | solution.py:24
  413.1 1.2 fusion.17
  414.3 1.3 convolution_subtract_fusion
  415.6 1.2 convolution_convert_fusion
  416.8 3.9 fusion.12
  420.7 197.6 %all-reduce.9.cloned.1.call-done = f32[256,6656]{1,0:T(8,128)} async-done(((f32[256,6656]{1,0:T(8,128)}), f32[256,6656]{1,0:T(8,128)}) %all-reduce.9.cloned.1.call-update) | async-done | bytes 6815760 | tf_op jit(solution)/shard_map/psum | solution.py:46
  618.3 3.6 multiply_reduce_fusion
  622.0 8.4 %psum.31 = f32[256]{0:T(256)S(1)} all-reduce(f32[256]{0:T(256)S(1)} %multiply_reduce_fusion), channel_id=1, replica_groups=mesh['fsdp'=64,'tensor'=4] {'tensor'}, use_global_device_ids=true, to_apply=%region_9.10 | all-reduce | flops 256 | bytes 2048 | tf_op jit(solution)/shard_map/psum | solution.py:47
  630.4 3.9 broadcast_divide_fusion
  634.3 2.8 fusion.2
  637.1 0.7 constant_dynamic-slice_fusion.1
  637.8 2.9 fusion.1
  (25 shorter events, 0.4 us)
Async XLA Ops:
  7.2 93.3 %copy-start = (bf16[256,6656]{1,0:T(8,128)(2,1)S(1)}, bf16[256,6656]{1,0:T(8,128)(2,1)}, u32[]{:S(2)}) copy-start(bf16[256,6656]{1,0:T(8,128)(2,1)} %param.2) | copy-start | bytes 10223620
  7.2 86.8 %all-gather.3.cloned.1.call-start = ((), (), s32[]{:S(2)}) async-start(), calls=%async_computation.3 | async-start | bytes 3461120 | tf_op jit(solution)/shard_map/all_gather | solution.py:36
  8.9 137.1 %all-reduce.5.cloned.1.call-start = ((), (), s32[]{:S(2)}) async-start(), calls=%async_computation | async-start | bytes 524288 | tf_op jit(solution)/shard_map/psum | solution.py:40
  104.3 224.2 %all-reduce.7.cloned.1.call-start = ((), (), s32[]{:S(2)}) async-start(), calls=%async_computation.1 | async-start | bytes 524288 | tf_op jit(solution)/shard_map/psum | solution.py:41
  148.4 469.9 %all-reduce.9.cloned.1.call-start = ((), (), s32[]{:S(2)}) async-start(), calls=%async_computation.2 | async-start | bytes 13631488 | tf_op jit(solution)/shard_map/psum | solution.py:46
  335.3 0.7 copy-start.2
  618.3 19.5 %slice-start = ((s8[6815744]{0:T(1024)(128)(4,1)}), s8[2621440]{0:T(1024)(128)(4,1)S(1)}, s32[]{:S(2)}) async-start(s8[6815744]{0:T(1024)(128)(4,1)} %bitcast.38), calls=%async_computation.4 | async-start | bytes 5242880
  630.4 7.4 %slice-start.1 = ((s8[6815744]{0:T(1024)(128)(4,1)}), s8[4194304]{0:T(1024)(128)(4,1)S(1)}, s32[]{:S(2)}) async-start(s8[6815744]{0:T(1024)(128)(4,1)} %bitcast.38), calls=%async_computation.5 | async-start | bytes 8388608
  634.3 3.5 copy-start.1
Sparse Core Ops, SparseCore 0:
  11.3 82.6 all-gather.2
  104.4 41.6 all-reduce.4
  150.5 177.9 all-reduce.6
  420.8 197.4 all-reduce.8
where the time goes:
time: 651 us; the launch traced here: 647 us
  waiting for transfers between devices  504 us (77%)
  other arithmetic  74.7 us (11%)
  matrix products  22.3 us (3%)
  local copies, waits for them, and re-layouts  21.5 us (3%)
  between operations  15.8 us (2%)
  blocking collectives  8.4 us (1%)
    psum x1, waiting for transfers between devices, per_device(): right_factor = lax.psum(right_local, 'fsdp')  198 us
    psum x1, waiting for transfers between devices, per_device(): gram_matrix = lax.psum(gram_of(projected), 'fsdp')  180 us
    all_gather x1, waiting for transfers between devices, per_device(): basis_whole = lax.all_gather(basis_half, 'fsdp', axis=0, tiled=True)  85 us
    psum x1, waiting for transfers between devices, per_device(): projected = lax.psum(partial_proj, 'tensor')  41.7 us
    another operation x6, other arithmetic, factor_of(): jnp.linalg.cholesky(gram_matrix + ridge * jnp.eye(width, dtype=jnp.float32))  38.3 us
    another operation x3, other arithmetic, orthonormalize(): lax.linalg.triangular_solve(factor, matrix, left_side=False, lower=True,...  22.8 us
  transfers between devices with their start and end apart: 4, of which 4 were waited for; matrix products, arithmetic and copies ran while one was open for 0% of the time, Pallas kernels for 0%

commit v1 on v0

v1 whole, which is shorter than its diff:
```python
import math

import jax
import jax.numpy as jnp
from jax import lax
from jax.sharding import Mesh
from jax.sharding import PartitionSpec as P

momentum_decay = 0.95
f32, bf16 = jnp.float32, jnp.bfloat16
HIGHEST = lax.Precision.HIGHEST


def swap_cores(block):
    return lax.ppermute(block, "c", [(0, 1), (1, 0)])


def gather(block, axes, parts):
    copies = jnp.broadcast_to(block[None], (parts,) + block.shape)
    return lax.all_to_all(copies, axes, 0, 0)


def scatter_sum(block, axes, parts):
    pieces = block.reshape((parts, block.shape[0] // parts) + block.shape[1:])
    return jnp.sum(lax.all_to_all(pieces, axes, 0, 0).astype(f32), axis=0)


def per_device(sizes, momentum, q_basis):
    nz, ny, nx = sizes
    rows, cols = momentum.shape
    half = cols // 2
    shard_rank = q_basis.shape[0]
    rank = shard_rank * nz * ny * 2
    core = lax.axis_index("c")

    def mine(array):
        return lax.dynamic_slice_in_dim(array, core * half, half, 1)

    def theirs(array):
        return lax.dynamic_slice_in_dim(array, (1 - core) * half, half, 1)

    def both(own, other):
        first = core == 0
        return jnp.concatenate([jnp.where(first, own, other), jnp.where(first, other, own)])

    basis_half = q_basis.astype(bf16)
    basis_chip = both(mine(basis_half), swap_cores(theirs(basis_half)))
    momentum_chip = both(mine(momentum), swap_cores(theirs(momentum)))

    basis_z = gather(basis_chip, "z", nz)
    basis_zy = gather(basis_z, "y", ny)
    basis_whole = basis_zy.transpose(1, 0, 2, 3).reshape(rank, half)
    partial_proj = lax.dot_general(
        momentum_chip, basis_whole, (((1,), (1,)), ((), ())), preferred_element_type=f32
    )
    proj_piece = scatter_sum(partial_proj, ("x", "c"), nx * 2)
    projected = gather(proj_piece, ("x", "c"), nx * 2).reshape(2 * rows, rank)

    gram_chip = jnp.dot(projected.T, projected, preferred_element_type=f32, precision=HIGHEST)
    place = lax.axis_index("x") * 2 + core
    part = rank // (nx * 2)
    gram_rows = lax.dynamic_slice_in_dim(gram_chip, place * part, part, 0)
    gram_rows = jnp.sum(gather(gram_rows, "y", ny), axis=0)
    gram_rows = jnp.sum(gather(gram_rows, "z", nz), axis=0)
    gram_matrix = gather(gram_rows, ("x", "c"), nx * 2).reshape(rank, rank)

    ridge = 0.001 * jnp.trace(gram_matrix) / rank
    factor = jnp.linalg.cholesky(gram_matrix + ridge * jnp.eye(rank, dtype=f32))
    solved = lax.linalg.triangular_solve(
        factor, projected, left_side=False, lower=True, transpose_a=True
    )
    orthonormal = solved.astype(bf16)

    right = lax.dot_general(
        momentum_chip, orthonormal, (((0,), (0,)), ((), ())), preferred_element_type=f32
    ).astype(bf16)
    right = scatter_sum(right, "y", ny).astype(bf16)
    right = scatter_sum(right, "z", nz).astype(bf16)
    right = gather(right, "z", nz).reshape(half // ny, rank)
    right = gather(right, "y", ny).reshape(half, rank)
    squares = lax.psum(jnp.sum(jnp.square(right.astype(f32)), axis=0), ("x", "c"))
    lengths = jnp.sqrt(squares + 1e-06)
    right_half = both(right, swap_cores(right))

    own_orth = lax.dynamic_slice_in_dim(orthonormal, core * rows, rows, 0)
    own_solved = lax.dynamic_slice_in_dim(solved, core * rows, rows, 0)
    total_rows = rows * nz * ny * 2
    total_cols = cols * nx
    scaling = math.sqrt(total_rows * total_cols / rank)
    scaled = (own_solved * (scaling / lengths)[None, :]).astype(bf16)

    def times_right(left):
        return lax.dot_general(
            left, right_half, (((1,), (1,)), ((), ())), preferred_element_type=f32
        )

    new_momentum = (
        momentum.astype(f32) - (1.0 - momentum_decay) * times_right(own_orth)
    ).astype(bf16)
    update = times_right(scaled).astype(bf16)
    position = (lax.axis_index("z") * ny + lax.axis_index("y")) * 2 + core
    first_row = position * shard_rank
    ranks = first_row + jnp.arange(shard_rank)
    picked = (ranks[:, None] == jnp.arange(rank)[None, :]).astype(bf16)
    own_lengths = lax.dynamic_slice_in_dim(lengths, first_row, shard_rank, 0)
    q_next = times_right(picked) / own_lengths[:, None]
    return (new_momentum, update, q_next)


def solution(mesh):
    nz, ny, nx = 8, 4, 4
    split = Mesh(mesh.devices.reshape(nz, ny, 2, nx), ("z", "y", "c", "x"))
    spec = P(("z", "y", "c"), "x")
    return jax.shard_map(
        lambda momentum, q_basis: per_device((nz, ny, nx), momentum, q_basis),
        mesh=split,
        in_specs=(spec, spec),
        out_specs=(spec, spec, spec),
        check_vma=False,
    )
```

time: 651 us -> 296 us (0.45)
  waiting for transfers between devices: 504 us -> 30.2 us
  blocking collectives: 8.4 us -> 142 us
  starting transfers between devices: 0.16 us -> 24.3 us
  between operations: 15.8 us -> 2.91 us
  other arithmetic: 74.7 us -> 63.1 us
  local copies, waits for them, and re-layouts: 21.5 us -> 13.3 us
    psum x3 -> x0, waiting for transfers between devices: 419 us -> none  [the longest x1 198 us: per_device(): right_factor = lax.psum(right_local, 'fsdp')]
    all_to_all x0 -> x8, blocking collectives: none -> 130 us  [the longest x5 75.1 us: gather(): return lax.all_to_all(copies, axes, 0, 0)]
    all_gather x1 -> x0, waiting for transfers between devices: 85 us -> none  [per_device(): basis_whole = lax.all_gather(basis_half, 'fsdp', axis=0, tiled=True)]
    all_to_all x0 -> x3, waiting for transfers between devices: none -> 30.2 us  [gather(): return lax.all_to_all(copies, axes, 0, 0)]
    all_to_all x0 -> x3, starting transfers between devices: none -> 15.5 us  [gather(): return lax.all_to_all(copies, axes, 0, 0)]
    ppermute x0 -> x3, starting transfers between devices: none -> 8.83 us  [swap_cores(): return lax.ppermute(block, 'c', [(0, 1), (1, 0)])]
    another operation x9, other arithmetic: 61.1 us -> 53.9 us  [the longest x6 33.9 us: per_device(): factor = jnp.linalg.cholesky(gram_matrix + ridge * jnp.eye(rank, dtype=f32))]
    another operation x18, local copies, waits for them, and re-layouts: 11.8 us -> 4.54 us
  transfers between devices with their start and end apart: 4 -> 6, of which waited for: 4 -> 3; matrix products, arithmetic and copies ran while one was open for 0% -> 3% of each run, Pallas kernels for 0% -> 0%
where the time goes in v1:
time: 296 us; the launch traced here: 295 us
  blocking collectives  142 us (48%)
  other arithmetic  63.1 us (21%)
  waiting for transfers between devices  30.2 us (10%)
  starting transfers between devices  24.3 us (8%)
  matrix products  18.7 us (6%)
  local copies, waits for them, and re-layouts  13.3 us (4%)
    all_to_all x5, blocking collectives, gather(): return lax.all_to_all(copies, axes, 0, 0)  75.1 us
    all_to_all x3, blocking collectives, scatter_sum(): return jnp.sum(lax.all_to_all(pieces, axes, 0, 0).astype(f32), axis=0)  55.3 us
    another operation x6, other arithmetic, per_device(): factor = jnp.linalg.cholesky(gram_matrix + ridge * jnp.eye(rank, dtype=f32))  33.9 us
    all_to_all x3, waiting for transfers between devices, gather(): return lax.all_to_all(copies, axes, 0, 0)  30.2 us
    another operation x3, other arithmetic, per_device(): lax.linalg.triangular_solve(factor, projected, left_side=False, lower=Tru...  19.9 us
    all_to_all x3, starting transfers between devices, gather(): return lax.all_to_all(copies, axes, 0, 0)  15.5 us
    dot_general x3, matrix products, times_right(): lax.dot_general(left, right_half, (((1,), (1,)), ((), ())), preferred_ele...  12.1 us
    psum x1, blocking collectives, per_device(): lax.psum(jnp.sum(jnp.square(right.astype(f32)), axis=0), ('x', 'c'))  11.8 us
  transfers between devices with their start and end apart: 6, of which 3 were waited for; matrix products, arithmetic and copies ran while one was open for 3% of the time, Pallas kernels for 0%

profile of v1, /device:TPU:1, one launch (start us, length us, event | category | flops | bytes accessed | tf_op | source)
XLA Modules:
  0.0 294.8 jit_solution(12733740164103008420)
XLA Ops:
  0.6 0.9 convert_element_type.32
  1.6 3.3 %collective-permute-start.1 = (bf16[4,3328]{1,0:T(4,128)(2,1)S(1)}, bf16[4,3328]{1,0:T(4,128)(2,1)S(1)}, u32[]{:S(2)}, u32[]{:S(2)}) collective-permute-start(bf16[4,3328]{1,0:T(4,128)(2,1)S(1)} %constant_dynamic-slice_fusion.2), channel_id=1, source_target_pairs={{0,4},{4,0},{1,5},{5,1},{2,6},{6,2},{3,7},{7,3},{8,12},{12,8},{9,1... | collective-permute-start | bytes 79880 | tf_op jit(solution)/shard_map/ppermute | solution.py:15
  4.9 1.6 constant_dynamic-slice_fusion.3
  6.7 20.6 %all_to_all.55 = bf16[8,8,3328]{2,1,0:T(8,128)(2,1)S(1)} all-to-all(bf16[8,8,3328]{2,1,0:T(8,128)(2,1)S(1)} %broadcast_in_dim.22), channel_id=1, replica_groups=mesh['z'=8,'y'=4,'c'=2,'x'=4] {'z'}, dimensions={0} | all-to-all | bytes 851968 | tf_op jit(solution)/shard_map/all_to_all | solution.py:20
  27.4 1.3 broadcast_in_dim.23
  28.7 4.2 %all-to-all-start.1 = ((bf16[4,8,8,3328]{3,2,1,0:T(8,128)(2,1)}), bf16[4,8,8,3328]{3,2,1,0:T(8,128)(2,1)S(1)}, u32[]{:S(2)}, u32[]{:S(2)}) async-start(bf16[4,8,8,3328]{3,2,1,0:T(8,128)(2,1)} %broadcast_in_dim.23), calls=%async_computation.1 | async-start | bytes 3407872 | tf_op jit(solution)/shard_map/all_to_all | solution.py:20
  32.8 2.5 broadcast_select_fusion.3
  35.4 1.2 copy-done
  36.6 2.0 pad_maximum_fusion
  38.5 14.2 %all-to-all-done.1 = bf16[4,8,8,3328]{3,2,1,0:T(8,128)(2,1)S(1)} async-done(((bf16[4,8,8,3328]{3,2,1,0:T(8,128)(2,1)}), bf16[4,8,8,3328]{3,2,1,0:T(8,128)(2,1)S(1)}, u32[]{:S(2)}, u32[]{:S(2)}) %all-to-all-start.1) | async-done | bytes 1703968 | tf_op jit(solution)/shard_map/all_to_all | solution.py:20
  52.9 1.8 copy-done.2
  54.7 1.1 fusion.25
  55.8 16.6 %all_to_all.56 = f32[8,64,256]{2,1,0:T(8,128)S(1)} all-to-all(f32[8,64,256]{2,1,0:T(8,128)S(1)} %fusion.25), channel_id=1, replica_groups=mesh['z'=8,'y'=4,'c'=2,'x'=4] {'x','c'}, dimensions={0} | all-to-all | bytes 1048576 | tf_op jit(solution)/shard_map/all_to_all | solution.py:25
  72.4 0.8 broadcast_in_dim.24
  73.3 4.4 %all-to-all-start.3 = ((f32[8,64,256]{2,1,0:T(8,128)}), f32[8,64,256]{2,1,0:T(8,128)S(1)}, u32[]{:S(2)}, u32[]{:S(2)}) async-start(f32[8,64,256]{2,1,0:T(8,128)} %broadcast_in_dim.24), calls=%async_computation.3 | async-start | bytes 1048576 | tf_op jit(solution)/shard_map/all_to_all | solution.py:20
  77.7 9.5 %all-to-all-done.3 = f32[8,64,256]{2,1,0:T(8,128)S(1)} async-done(((f32[8,64,256]{2,1,0:T(8,128)}), f32[8,64,256]{2,1,0:T(8,128)S(1)}, u32[]{:S(2)}, u32[]{:S(2)}) %all-to-all-start.3) | async-done | bytes 524320 | tf_op jit(solution)/shard_map/all_to_all | solution.py:20
  87.2 1.0 convolution_bitcast_fusion
  88.3 7.2 %all_to_all.57 = f32[4,32,256]{2,1,0:T(8,128)S(1)} all-to-all(f32[4,32,256]{2,1,0:T(8,128)S(1)} %broadcast_in_dim.26), channel_id=1, replica_groups=mesh['z'=8,'y'=4,'c'=2,'x'=4] {'y'}, dimensions={0} | all-to-all | bytes 262144 | tf_op jit(solution)/shard_map/all_to_all | solution.py:20
  95.5 11.7 %all_to_all.58 = f32[8,32,256]{2,1,0:T(8,128)S(1)} all-to-all(f32[8,32,256]{2,1,0:T(8,128)S(1)} %broadcast_in_dim.28), channel_id=1, replica_groups=mesh['z'=8,'y'=4,'c'=2,'x'=4] {'z'}, dimensions={0} | all-to-all | bytes 524288 | tf_op jit(solution)/shard_map/all_to_all | solution.py:20
  107.3 0.7 broadcast_in_dim.29
  108.0 6.8 %all-to-all-start.6 = ((f32[8,32,256]{2,1,0:T(8,128)}), f32[8,32,256]{2,1,0:T(8,128)S(1)}, u32[]{:S(2)}, u32[]{:S(2)}) async-start(f32[8,32,256]{2,1,0:T(8,128)} %broadcast_in_dim.29), calls=%async_computation.6 | async-start | bytes 524288 | tf_op jit(solution)/shard_map/all_to_all | solution.py:20
  114.8 6.5 %all-to-all-done.6 = f32[8,32,256]{2,1,0:T(8,128)S(1)} async-done(((f32[8,32,256]{2,1,0:T(8,128)}), f32[8,32,256]{2,1,0:T(8,128)S(1)}, u32[]{:S(2)}, u32[]{:S(2)}) %all-to-all-start.6) | async-done | bytes 262176 | tf_op jit(solution)/shard_map/all_to_all | solution.py:20
  121.5 0.7 select_reduce_fusion
  123.1 11.7 %cholesky.49 = f32[128,128]{1,0:T(8,128)S(1)} custom-call(f32[128,128]{1,0:T(8,128)S(1)} %cholesky.115), custom_call_target="Cholesky" | custom-call | tf_op jit(solution)/shard_map/jit(cholesky)/cholesky | solution.py:68
  135.0 9.8 %custom-call.14 = f32[1,128,128]{1,2,0:T(8,128)S(1)} custom-call(f32[1,128,128]{2,1,0:T(8,128)S(1)} %get-tuple-element.44), custom_call_target="InvertDiagBlocksLowerTriangular" | custom-call | tf_op jit(solution)/shard_map/jit(cholesky)/cholesky | solution.py:68
  145.4 11.7 %cholesky.103 = f32[128,128]{1,0:T(8,128)S(1)} custom-call(f32[128,128]{1,0:T(8,128)S(1)} %convolution_subtract_fusion.1), custom_call_target="Cholesky" | custom-call | tf_op jit(solution)/shard_map/jit(cholesky)/cholesky | solution.py:68
  157.2 0.6 compare_reduce_fusion
  159.3 4.2 %while.1 = (s32[]{:T(128)}, f32[256,256]{0,1:T(8,128)S(1)}, s32[2,2]{1,0:T(2,128)S(1)}, f32[2,128,128]{2,1,0:T(8,128)S(1)}, s32[]{:T(128)}) while((s32[]{:T(128)}, f32[256,256]{0,1:T(8,128)S(1)}, s32[2,2]{1,0:T(2,128)S(1)}, f32[2,128,128]{2,1,0:T(8,128)S(1)}, s32[]{:T(128)}) %tuple.33), condition=%wide.while_cond, body=%wide.while_body.sunk | while | flops 2 | bytes 393329 | solution.py:69
  159.3 0.6 fusion.36
  159.9 1.4 dynamic-slice.7
  161.5 0.6 fusion.36
  162.0 1.4 dynamic-slice.7
  163.6 19.9 %custom-call.15 = f32[2,128,128]{1,2,0:T(8,128)S(1)} custom-call(f32[2,128,128]{2,1,0:T(8,128)S(1)} %get-tuple-element.10), custom_call_target="InvertDiagBlocksLowerTriangular" | custom-call | tf_op jit(solution)/shard_map/triangular_solve | solution.py:69
  183.9 0.6 convolution_subtract_fusion
  184.9 2.6 convolution_convert_fusion.1
  187.5 23.6 %all_to_all.59 = bf16[4,832,256]{2,1,0:T(8,128)(2,1)S(1)} all-to-all(bf16[4,832,256]{2,1,0:T(8,128)(2,1)S(1)} %bitcast.56), channel_id=1, replica_groups=mesh['z'=8,'y'=4,'c'=2,'x'=4] {'y'}, dimensions={0} | all-to-all | bytes 3407872 | tf_op jit(solution)/shard_map/all_to_all | solution.py:25
  211.1 0.5 reduce_sum.74
  211.6 15.2 %all_to_all.60 = bf16[8,104,256]{2,1,0:T(8,128)(2,1)S(1)} all-to-all(bf16[8,104,256]{2,1,0:T(8,128)(2,1)S(1)} %bitcast.57), channel_id=1, replica_groups=mesh['z'=8,'y'=4,'c'=2,'x'=4] {'z'}, dimensions={0} | all-to-all | bytes 851968 | tf_op jit(solution)/shard_map/all_to_all | solution.py:25
  226.8 15.4 %all_to_all.61 = bf16[8,104,256]{2,1,0:T(8,128)(2,1)S(1)} all-to-all(bf16[8,104,256]{2,1,0:T(8,128)(2,1)S(1)} %broadcast_in_dim.31), channel_id=1, replica_groups=mesh['z'=8,'y'=4,'c'=2,'x'=4] {'z'}, dimensions={0} | all-to-all | bytes 851968 | tf_op jit(solution)/shard_map/all_to_all | solution.py:20
  242.3 20.1 %all_to_all.62 = bf16[4,832,256]{2,1,0:T(8,128)(2,1)S(1)} all-to-all(bf16[4,832,256]{2,1,0:T(8,128)(2,1)S(1)} %broadcast_in_dim.33), channel_id=1, replica_groups=mesh['z'=8,'y'=4,'c'=2,'x'=4] {'y'}, dimensions={0} | all-to-all | bytes 3407872 | tf_op jit(solution)/shard_map/all_to_all | solution.py:20
  262.5 5.4 %collective-permute-start.2 = (bf16[3328,256]{1,0:T(8,128)(2,1)S(1)}, bf16[3328,256]{1,0:T(8,128)(2,1)}, u32[]{:S(2)}, u32[]{:S(2)}) collective-permute-start(bf16[3328,256]{1,0:T(8,128)(2,1)S(1)} %bitcast.49), channel_id=1, source_target_pairs={{0,4},{4,0},{1,5},{5,1},{2,6},{6,2},{3,7},{7,3},{8,12},{12,8},{9,1... | collective-permute-start | bytes 5111816 | tf_op jit(solution)/shard_map/ppermute | solution.py:15
  267.9 0.5 multiply_reduce_fusion
  268.3 11.8 %psum.7 = f32[256]{0:T(256)S(1)} all-reduce(f32[256]{0:T(256)S(1)} %multiply_reduce_fusion), channel_id=1, replica_groups=mesh['z'=8,'y'=4,'c'=2,'x'=4] {'x','c'}, use_global_device_ids=true, to_apply=%region_11.12 | all-reduce | flops 256 | bytes 2048 | tf_op jit(solution)/shard_map/psum | solution.py:81
  280.2 1.8 broadcast_select_fusion.1
  282.0 0.6 copy-done.1
  282.7 7.6 %fusion.1 = bf16[256,6656]{1,0:T(8,128)(2,1)} fusion(bf16[256,6656]{1,0:T(8,128)(2,1)S(1)} %copy-done.1, bf16[3328,256]{1,0:T(8,128)(2,1)S(1)} %get-tuple-element.40, bf16[3328,256]{1,0:T(8,128)(2,1)S(1)} %get-tuple-element.39, bf16[512,256]{0,1:T(8,128)(2,1)S(1)} %fusion.2, s32[]{:T(128)S(6)} %select_n.75), kind=kOutput, calls=%fused_computation.5 | convolution fusion | flops 886046720 | bytes 10354692 | tf_op jit(solution)/shard_map/dot_general | solution.py:93
  290.2 2.9 convolution_convert_fusion
  293.2 1.6 convolution_divide_fusion
  (53 shorter events, 3.1 us)
Async XLA Ops:
  1.6 5.0 %collective-permute-start.1 = (bf16[4,3328]{1,0:T(4,128)(2,1)S(1)}, bf16[4,3328]{1,0:T(4,128)(2,1)S(1)}, u32[]{:S(2)}, u32[]{:S(2)}) collective-permute-start(bf16[4,3328]{1,0:T(4,128)(2,1)S(1)} %constant_dynamic-slice_fusion.2), channel_id=1, source_target_pairs={{0,4},{4,0},{1,5},{5,1},{2,6},{6,2},{3,7},{7,3},{8,12},{12,8},{9,1... | collective-permute-start | bytes 79880 | tf_op jit(solution)/shard_map/ppermute | solution.py:15
  6.5 26.4 %collective-permute-start = (bf16[256,3328]{1,0:T(8,128)(2,1)S(1)}, bf16[256,3328]{1,0:T(8,128)(2,1)}, u32[]{:S(2)}, u32[]{:S(2)}) collective-permute-start(bf16[256,3328]{1,0:T(8,128)(2,1)S(1)} %constant_dynamic-slice_fusion.3), channel_id=1, source_target_pairs={{0,4},{4,0},{1,5},{5,1},{2,6},{6,2},{3,7},{7,3},{8,12},{12,8},{9,1... | collective-permute-start | bytes 5111816 | tf_op jit(solution)/shard_map/ppermute | solution.py:15
  28.7 24.1 %all-to-all-start.1 = ((bf16[4,8,8,3328]{3,2,1,0:T(8,128)(2,1)}), bf16[4,8,8,3328]{3,2,1,0:T(8,128)(2,1)S(1)}, u32[]{:S(2)}, u32[]{:S(2)}) async-start(bf16[4,8,8,3328]{3,2,1,0:T(8,128)(2,1)} %broadcast_in_dim.23), calls=%async_computation.1 | async-start | bytes 3407872 | tf_op jit(solution)/shard_map/all_to_all | solution.py:20
  35.4 1.2 copy-start
  52.8 2.0 copy-start.2
  73.3 13.9 %all-to-all-start.3 = ((f32[8,64,256]{2,1,0:T(8,128)}), f32[8,64,256]{2,1,0:T(8,128)S(1)}, u32[]{:S(2)}, u32[]{:S(2)}) async-start(f32[8,64,256]{2,1,0:T(8,128)} %broadcast_in_dim.24), calls=%async_computation.3 | async-start | bytes 1048576 | tf_op jit(solution)/shard_map/all_to_all | solution.py:20
  108.0 13.4 %all-to-all-start.6 = ((f32[8,32,256]{2,1,0:T(8,128)}), f32[8,32,256]{2,1,0:T(8,128)S(1)}, u32[]{:S(2)}, u32[]{:S(2)}) async-start(f32[8,32,256]{2,1,0:T(8,128)} %broadcast_in_dim.29), calls=%async_computation.6 | async-start | bytes 524288 | tf_op jit(solution)/shard_map/all_to_all | solution.py:20
  262.5 17.7 %collective-permute-start.2 = (bf16[3328,256]{1,0:T(8,128)(2,1)S(1)}, bf16[3328,256]{1,0:T(8,128)(2,1)}, u32[]{:S(2)}, u32[]{:S(2)}) collective-permute-start(bf16[3328,256]{1,0:T(8,128)(2,1)S(1)} %bitcast.49), channel_id=1, source_target_pairs={{0,4},{4,0},{1,5},{5,1},{2,6},{6,2},{3,7},{7,3},{8,12},{12,8},{9,1... | collective-permute-start | bytes 5111816 | tf_op jit(solution)/shard_map/ppermute | solution.py:15
  280.2 2.5 copy-start.1

commit v2 on v1

v2 whole, which is shorter than its diff:
```python
import math

import jax
import jax.numpy as jnp
from jax import lax
from jax.experimental import pallas as pl
from jax.experimental.pallas import tpu as pltpu
from jax.sharding import Mesh
from jax.sharding import PartitionSpec as P

momentum_decay = 0.95
f32, bf16 = jnp.float32, jnp.bfloat16
HIGHEST = lax.Precision.HIGHEST
VMEM = pl.BlockSpec(memory_space=pltpu.VMEM)
PIVOTS = 8


def inverse_factor_kernel(gram_ref, inverse_ref, work_ref):
    rank = gram_ref.shape[0]
    gram = gram_ref[...]
    diagonal = lax.broadcasted_iota(jnp.int32, gram.shape, 0) == lax.broadcasted_iota(
        jnp.int32, gram.shape, 1
    )
    ridge = 0.001 * jnp.sum(jnp.where(diagonal, gram, 0.0)) / rank
    work_ref[...] = jnp.where(diagonal, gram + ridge, gram)
    lane = lax.broadcasted_iota(jnp.int32, (1, rank), 1)

    def wide(value):
        return jnp.concatenate([value] * (rank // 128), axis=1)

    steps = range(PIVOTS)
    for start in range(0, rank, PIVOTS):
        end = start + PIVOTS
        block = work_ref[start:end, :]
        spread = [jnp.broadcast_to(block[:, start + t : start + t + 1], (PIVOTS, 128)) for t in steps]
        core = [[spread[t][s : s + 1, :] for t in range(s + 1)] for s in steps]
        inside = (lane >= start) & (lane < end)
        row = [
            jnp.where(inside, (lane == start + s).astype(f32), block[s : s + 1, :]) for s in steps
        ]
        inverse = [None] * PIVOTS
        ratio = [[None] * PIVOTS for _ in steps]
        for t in steps:
            inverse[t] = 1.0 / core[t][t]
            for s in range(t + 1, PIVOTS):
                ratio[s][t] = core[s][t] * inverse[t]
            for s in range(t + 1, PIVOTS):
                for u in range(t + 1, s + 1):
                    core[s][u] = core[s][u] - ratio[s][t] * core[u][t]
                row[s] = row[s] - wide(ratio[s][t]) * row[t]
        for s in steps:
            scaled = row[s] * wide(lax.rsqrt(core[s][s]))
            inverse_ref[start + s : start + s + 1, :] = jnp.where(lane < end, scaled, 0.0)
        if end < rank:
            solved = [row[s] * wide(inverse[s]) for s in steps]
            for s in reversed(steps):
                for t in range(s):
                    solved[t] = solved[t] - wide(ratio[s][t]) * solved[s]
            below = work_ref[end:, :]
            rest = jnp.where(inside, 0.0, below)
            for t in steps:
                rest = rest - below[:, start + t : start + t + 1] * solved[t]
            work_ref[end:, :] = rest


def inverse_factor(gram_matrix):
    return pl.pallas_call(
        inverse_factor_kernel,
        out_shape=jax.ShapeDtypeStruct(gram_matrix.shape, f32),
        in_specs=[VMEM],
        out_specs=VMEM,
        scratch_shapes=[pltpu.VMEM(gram_matrix.shape, f32)],
        compiler_params=pltpu.CompilerParams(vmem_limit_bytes=8 * 2**20),
    )(gram_matrix)


def cross_kernel(momentum_ref, terms_ref, out_ref):
    rank = out_ref.shape[1]
    product = lax.dot_general(
        momentum_ref[...], terms_ref[...], (((0,), (0,)), ((), ())), preferred_element_type=f32
    )
    out_ref[...] = (
        product[:, 2 * rank :] + product[:, rank : 2 * rank] + product[:, :rank]
    )


def cross(momentum, projected):
    rows, cols = momentum.shape
    rank = projected.shape[1]
    high = lax.reduce_precision(projected, 8, 7)
    left = projected - high
    middle = lax.reduce_precision(left, 8, 7)
    low = left - middle
    terms = jnp.concatenate([high, middle, low], axis=1).astype(bf16)
    block = 256
    return pl.pallas_call(
        cross_kernel,
        out_shape=jax.ShapeDtypeStruct((cols, rank), f32),
        grid=(cols // block,),
        in_specs=[
            pl.BlockSpec((rows, block), lambda i: (0, i)),
            pl.BlockSpec((rows, 3 * rank), lambda i: (0, 0)),
        ],
        out_specs=pl.BlockSpec((block, rank), lambda i: (i, 0)),
        compiler_params=pltpu.CompilerParams(vmem_limit_bytes=16 * 2**20),
        cost_estimate=pl.CostEstimate(
            flops=6 * rows * cols * rank, bytes_accessed=2 * rows * cols + 4 * cols * rank, transcendentals=0
        ),
    )(momentum, terms)


def swap_cores(block):
    return lax.ppermute(block, "c", [(0, 1), (1, 0)])


def shift(block, axis, parts, by):
    return lax.ppermute(block, axis, [(i, (i + by) % parts) for i in range(parts)])


def sum_four(block, axis):
    right, across, left = (shift(block, axis, 4, by) for by in (1, 2, 3))
    return (block + across) + (right + left)


def gather(block, axes, parts):
    copies = jnp.broadcast_to(block[None], (parts,) + block.shape)
    return lax.all_to_all(copies, axes, 0, 0)


def scatter_sum(block, axes, parts):
    pieces = block.reshape((parts, block.shape[0] // parts) + block.shape[1:])
    return jnp.sum(lax.all_to_all(pieces, axes, 0, 0).astype(f32), axis=0)


def per_device(sizes, momentum, q_basis):
    nz, ny, nx = sizes
    rows, cols = momentum.shape
    half = cols // 2
    shard_rank = q_basis.shape[0]
    rank = shard_rank * nz * ny * 2
    core = lax.axis_index("c")

    def mine(array):
        return lax.dynamic_slice_in_dim(array, core * half, half, 1)

    def theirs(array):
        return lax.dynamic_slice_in_dim(array, (1 - core) * half, half, 1)

    def both(own, other):
        first = core == 0
        return jnp.concatenate([jnp.where(first, own, other), jnp.where(first, other, own)])

    basis_half = q_basis.astype(bf16)
    basis_chip = both(mine(basis_half), swap_cores(theirs(basis_half)))
    momentum_chip = both(mine(momentum), swap_cores(theirs(momentum)))

    basis_z = gather(basis_chip, "z", nz)
    basis_zy = gather(basis_z, "y", ny)
    basis_whole = basis_zy.transpose(1, 0, 2, 3).reshape(rank, half)
    partial_proj = lax.dot_general(
        momentum_chip, basis_whole, (((1,), (1,)), ((), ())), preferred_element_type=f32
    )
    proj_own = lax.dynamic_slice_in_dim(partial_proj, core * rows, rows, 0)
    proj_other = lax.dynamic_slice_in_dim(partial_proj, (1 - core) * rows, rows, 0)
    projected = sum_four(proj_own + swap_cores(proj_other), "x")

    gram_own = jnp.dot(projected.T, projected, preferred_element_type=f32, precision=HIGHEST)
    place = lax.axis_index("x") * 2
    part = rank // (nx * 2)
    gram_keep = lax.dynamic_slice_in_dim(gram_own, (place + core) * part, part, 0)
    gram_send = lax.dynamic_slice_in_dim(gram_own, (place + 1 - core) * part, part, 0)
    gram_rows = sum_four(gram_keep + swap_cores(gram_send), "y")
    gram_rows = jnp.sum(gather(gram_rows, "z", nz), axis=0)
    gram_matrix = gather(gram_rows, ("x", "c"), nx * 2).reshape(rank, rank)

    right = cross(momentum_chip, both(projected, swap_cores(projected)))
    piece = half // ny
    at_y = lax.axis_index("y")
    pieces = [
        lax.dynamic_slice_in_dim(right, lax.rem(at_y + by, ny) * piece, piece, 0) for by in range(ny)
    ]
    right = pieces[0] + sum(shift(pieces[by], "y", ny, by) for by in range(1, ny))

    inverse = inverse_factor(gram_matrix)

    def whiten(array):
        return lax.dot_general(
            array, inverse, (((1,), (1,)), ((), ())), preferred_element_type=f32, precision=HIGHEST
        )

    solved = whiten(projected)
    orthonormal = solved.astype(bf16)
    right = scatter_sum(whiten(right).astype(bf16), "z", nz).astype(bf16)
    right = gather(right, "z", nz).reshape(piece, rank)
    right = gather(right, "y", ny).reshape(half, rank)
    squares = jnp.sum(jnp.square(right.astype(f32)), axis=0, keepdims=True)
    squares = sum_four(squares + swap_cores(squares), "x")
    lengths = jnp.sqrt(squares + 1e-06)
    right_half = both(right, swap_cores(right))

    total_rows = rows * nz * ny * 2
    total_cols = cols * nx
    scaling = math.sqrt(total_rows * total_cols / rank)
    scaled = (solved * (scaling / lengths)).astype(bf16)

    def times_right(left):
        return lax.dot_general(
            left, right_half, (((1,), (1,)), ((), ())), preferred_element_type=f32
        )

    new_momentum = (
        momentum.astype(f32) - (1.0 - momentum_decay) * times_right(orthonormal)
    ).astype(bf16)
    update = times_right(scaled).astype(bf16)
    position = (lax.axis_index("z") * ny + lax.axis_index("y")) * 2 + core
    first_row = position * shard_rank
    ranks = first_row + jnp.arange(shard_rank)
    picked = (ranks[:, None] == jnp.arange(rank)[None, :]).astype(bf16)
    own_lengths = lax.dynamic_slice_in_dim(lengths[0], first_row, shard_rank, 0)
    q_next = times_right(picked) / own_lengths[:, None]
    return (new_momentum, update, q_next)


def solution(mesh):
    nz, ny, nx = 8, 4, 4
    split = Mesh(mesh.devices.reshape(nz, ny, 2, nx), ("z", "y", "c", "x"))
    spec = P(("z", "y", "c"), "x")
    return jax.shard_map(
        lambda momentum, q_basis: per_device((nz, ny, nx), momentum, q_basis),
        mesh=split,
        in_specs=(spec, spec),
        out_specs=(spec, spec, spec),
        check_vma=False,
    )
```

time: 296 us -> 223 us (0.75)
  blocking collectives: 142 us -> 85.8 us
  other arithmetic: 63.1 us -> 11.5 us
  Pallas kernels: 0 us -> 16.4 us
  starting transfers between devices: 24.3 us -> 38.5 us
  waiting for transfers between devices: 30.2 us -> 43.1 us
  local copies, waits for them, and re-layouts: 13.3 us -> 9.03 us
    another operation x9 -> x1, other arithmetic: 53.9 us -> 0.12 us  [the longest x6 33.9 us: per_device(): factor = jnp.linalg.cholesky(gram_matrix + ridge * jnp.eye(rank, dtype=f32))]
    all_to_all x3 -> x1, blocking collectives: 55.3 us -> 16.8 us  [scatter_sum(): return jnp.sum(lax.all_to_all(pieces, axes, 0, 0).astype(f32), axis=0)]
    pallas_call x0 -> x2, Pallas kernels: none -> 16.4 us  [the longest x1 10.7 us: inverse_factor(): pl.pallas_call(inverse_factor_kernel, out_shape=jax.ShapeDtypeStruct(gram...]
    ppermute x0 -> x12, waiting for transfers between devices: none -> 14.9 us  [shift(): lax.ppermute(block, axis, [(i, (i + by) % parts) for i in range(parts)])]
    ppermute x0 -> x12, starting transfers between devices: none -> 14 us  [shift(): lax.ppermute(block, axis, [(i, (i + by) % parts) for i in range(parts)])]
    psum x1 -> x0, blocking collectives: 11.8 us -> none  [per_device(): lax.psum(jnp.sum(jnp.square(right.astype(f32)), axis=0), ('x', 'c'))]
    all_to_all x3 -> x2, waiting for transfers between devices: 30.2 us -> 23.1 us  [gather(): return lax.all_to_all(copies, axes, 0, 0)]
    all_to_all x5 -> x4, blocking collectives: 75.1 us -> 69 us  [gather(): return lax.all_to_all(copies, axes, 0, 0)]
  transfers between devices with their start and end apart: 6 -> 21, of which waited for: 3 -> 9; matrix products, arithmetic and copies ran while one was open for 3% -> 5% of each run, Pallas kernels for 0% -> 7%
where the time goes in v2:
time: 223 us; the launch traced here: 222 us
  blocking collectives  85.8 us (38%)
  waiting for transfers between devices  43.1 us (19%)
  starting transfers between devices  38.5 us (17%)
  matrix products  16.8 us (8%)
  Pallas kernels  16.4 us (7%)
  other arithmetic  11.5 us (5%)
  local copies, waits for them, and re-layouts  9.03 us (4%)
    all_to_all x4, blocking collectives, gather(): return lax.all_to_all(copies, axes, 0, 0)  69 us
    all_to_all x2, waiting for transfers between devices, gather(): return lax.all_to_all(copies, axes, 0, 0)  23.1 us
    all_to_all x1, blocking collectives, scatter_sum(): return jnp.sum(lax.all_to_all(pieces, axes, 0, 0).astype(f32), axis=0)  16.8 us
    ppermute x12, waiting for transfers between devices, shift(): lax.ppermute(block, axis, [(i, (i + by) % parts) for i in range(parts)])  14.9 us
    ppermute x12, starting transfers between devices, shift(): lax.ppermute(block, axis, [(i, (i + by) % parts) for i in range(parts)])  14 us
    ppermute x7, starting transfers between devices, swap_cores(): return lax.ppermute(block, 'c', [(0, 1), (1, 0)])  12.8 us
    dot_general x3, matrix products, times_right(): lax.dot_general(left, right_half, (((1,), (1,)), ((), ())), preferred_ele...  12.1 us
    all_to_all x2, starting transfers between devices, gather(): return lax.all_to_all(copies, axes, 0, 0)  11.7 us
  transfers between devices with their start and end apart: 21, of which 9 were waited for; matrix products, arithmetic and copies ran while one was open for 5% of the time, Pallas kernels for 7%

profile of v2, /device:TPU:1, one launch (start us, length us, event | category | flops | bytes accessed | tf_op | source)
XLA Modules:
  0.0 222.1 jit_solution(2580464959576558327)
XLA Ops:
  0.6 0.9 convert_element_type.30
  1.6 3.3 %collective-permute-start.1 = (bf16[4,3328]{1,0:T(4,128)(2,1)S(1)}, bf16[4,3328]{1,0:T(4,128)(2,1)S(1)}, u32[]{:S(2)}, u32[]{:S(2)}) collective-permute-start(bf16[4,3328]{1,0:T(4,128)(2,1)S(1)} %constant_dynamic-slice_fusion.6), channel_id=1, source_target_pairs={{0,4},{4,0},{1,5},{5,1},{2,6},{6,2},{3,7},{7,3},{8,12},{12,8},{9,1... | collective-permute-start | bytes 79880 | tf_op jit(solution)/shard_map/ppermute | solution.py:113
  4.9 1.6 constant_dynamic-slice_fusion.7
  6.7 20.6 %all_to_all.35 = bf16[8,8,3328]{2,1,0:T(8,128)(2,1)S(1)} all-to-all(bf16[8,8,3328]{2,1,0:T(8,128)(2,1)S(1)} %broadcast_in_dim.16), channel_id=1, replica_groups=mesh['z'=8,'y'=4,'c'=2,'x'=4] {'z'}, dimensions={0} | all-to-all | bytes 851968 | tf_op jit(solution)/shard_map/all_to_all | solution.py:127
  27.4 1.3 broadcast_in_dim.17
  28.7 4.2 %all-to-all-start.1 = ((bf16[4,8,8,3328]{3,2,1,0:T(8,128)(2,1)}), bf16[4,8,8,3328]{3,2,1,0:T(8,128)(2,1)S(1)}, u32[]{:S(2)}, u32[]{:S(2)}) async-start(bf16[4,8,8,3328]{3,2,1,0:T(8,128)(2,1)} %broadcast_in_dim.17), calls=%async_computation.1 | async-start | bytes 3407872 | tf_op jit(solution)/shard_map/all_to_all | solution.py:127
  32.8 3.7 %broadcast_select_fusion.3 = (bf16[256,3328]{1,0:T(8,128)(2,1)S(1)}, bf16[256,3328]{1,0:T(8,128)(2,1)}) fusion(bf16[256,3328]{1,0:T(8,128)(2,1)} %collective-permute-done, pred[]{:T(512)S(6)} %eq.8, bf16[256,6656]{1,0:T(8,128)(2,1)} %param.2, s32[]{:T(128)S(6)} %select_n.84), kind=kLoop, calls=%fused_computation.11 | loop fusion | flops 1703936 | bytes 6815749 | tf_op jit(solution)/shard_map/jit(_where)/select_n | solution.py:151
  36.5 16.2 %all-to-all-done.1 = bf16[4,8,8,3328]{3,2,1,0:T(8,128)(2,1)S(1)} async-done(((bf16[4,8,8,3328]{3,2,1,0:T(8,128)(2,1)}), bf16[4,8,8,3328]{3,2,1,0:T(8,128)(2,1)S(1)}, u32[]{:S(2)}, u32[]{:S(2)}) %all-to-all-start.1) | async-done | bytes 1703968 | tf_op jit(solution)/shard_map/all_to_all | solution.py:127
  52.9 1.3 copy-done.2
  54.2 1.1 fusion.15
  55.3 0.8 copy-done.7
  56.1 0.7 constant_dynamic-slice_fusion.5
  56.8 3.1 %collective-permute-start.2 = (f32[256,256]{1,0:T(8,128)}, f32[256,256]{1,0:T(8,128)}, u32[]{:S(2)}, u32[]{:S(2)}) collective-permute-start(f32[256,256]{1,0:T(8,128)} %constant_dynamic-slice_fusion.5), channel_id=1, source_target_pairs={{0,4},{4,0},{1,5},{5,1},{2,6},{6,2},{3,7},{7,3},{8,12},{12,8},{9,1... | collective-permute-start | bytes 786440 | tf_op jit(solution)/shard_map/ppermute | solution.py:113
  60.0 1.5 collective-permute-done.2
  61.5 1.8 dynamic-slice_add_fusion
  63.2 1.2 collective-permute-start.4
  64.4 1.5 collective-permute-start.5
  65.9 1.5 collective-permute-start.3
  67.4 4.8 %collective-permute-done.4 = f32[256,256]{1,0:T(8,128)} collective-permute-done((f32[256,256]{1,0:T(8,128)}, f32[256,256]{1,0:T(8,128)}, u32[]{:S(2)}, u32[]{:S(2)}) %collective-permute-start.4) | collective-permute-done | bytes 262176 | tf_op jit(solution)/shard_map/ppermute | solution.py:117
  72.3 6.6 %collective-permute-done.3 = f32[256,256]{1,0:T(8,128)} collective-permute-done((f32[256,256]{1,0:T(8,128)}, f32[256,256]{1,0:T(8,128)}, u32[]{:S(2)}, u32[]{:S(2)}) %collective-permute-start.3) | collective-permute-done | bytes 262176 | tf_op jit(solution)/shard_map/ppermute | solution.py:117
  78.9 1.3 add_add_fusion
  80.1 0.6 fusion.16
  80.7 1.3 collective-permute-start.10
  82.4 0.9 collective-permute-done.6
  83.5 2.4 %collective-permute-start.9 = (f32[32,256]{1,0:T(8,128)S(1)}, f32[32,256]{1,0:T(8,128)S(1)}, u32[]{:S(2)}, u32[]{:S(2)}) collective-permute-start(f32[32,256]{1,0:T(8,128)S(1)} %dynamic-slice_add_fusion.1), channel_id=1, source_target_pairs={{0,24},{8,0},{16,8},{24,16},{1,25},{9,1},{17,9},{25,17},{2,26},{10... | collective-permute-start | bytes 98312 | tf_op jit(solution)/shard_map/ppermute | solution.py:117
  86.2 5.7 %shard_map.50 = f32[3328,256]{1,0:T(8,128)S(1)} custom-call(bf16[512,3328]{1,0:T(8,128)(2,1)S(1)} %pad_maximum_fusion.momentum_ref, bf16[512,768]{1,0:T(8,128)(2,1)S(1)} %pad_maximum_fusion.5.terms_ref), custom_call_target="tpu_custom_call" | custom-call | flops 2617245696 | bytes 6815744 | tf_op jit(solution)/shard_map/pallas_call | solution.py:96
  91.9 1.6 constant_dynamic-slice_fusion.2
  93.5 1.5 collective-permute-start.13
  94.9 3.0 %collective-permute-start.12 = (f32[832,256]{1,0:T(8,128)}, f32[832,256]{1,0:T(8,128)}, u32[]{:S(2)}, u32[]{:S(2)}) collective-permute-start(f32[832,256]{1,0:T(8,128)} %get-tuple-element.9), channel_id=1, source_target_pairs={{0,16},{8,24},{16,0},{24,8},{1,17},{9,25},{17,1},{25,9},{2,18},{10... | collective-permute-start | bytes 2555912 | tf_op jit(solution)/shard_map/ppermute | solution.py:117
  97.9 12.2 %all_to_all.36 = f32[8,32,256]{2,1,0:T(8,128)} all-to-all(f32[8,32,256]{2,1,0:T(8,128)S(1)} %broadcast_in_dim.18), channel_id=1, replica_groups=mesh['z'=8,'y'=4,'c'=2,'x'=4] {'z'}, dimensions={0} | all-to-all | bytes 524288 | tf_op jit(solution)/shard_map/all_to_all | solution.py:127
  110.2 1.0 reduce_sum.30
  111.2 0.7 broadcast_in_dim.19
  111.9 7.6 %all-to-all-start.3 = ((f32[8,32,256]{2,1,0:T(8,128)}), f32[8,32,256]{2,1,0:T(8,128)}, u32[]{:S(2)}, u32[]{:S(2)}) async-start(f32[8,32,256]{2,1,0:T(8,128)} %broadcast_in_dim.19), calls=%async_computation.3 | async-start | bytes 524288 | tf_op jit(solution)/shard_map/all_to_all | solution.py:127
  119.4 6.9 %all-to-all-done.3 = f32[8,32,256]{2,1,0:T(8,128)} async-done(((f32[8,32,256]{2,1,0:T(8,128)}), f32[8,32,256]{2,1,0:T(8,128)}, u32[]{:S(2)}, u32[]{:S(2)}) %all-to-all-start.3) | async-done | bytes 262176 | tf_op jit(solution)/shard_map/all_to_all | solution.py:127
  126.3 10.7 %shard_map.49 = f32[256,256]{1,0:T(8,128)S(1)} custom-call(f32[256,256]{1,0:T(8,128)} %bitcast.2.gram_ref), custom_call_target="tpu_custom_call" | custom-call | tf_op jit(solution)/shard_map/pallas_call | solution.py:67
  137.1 2.6 %convolution_convert_fusion.1 = bf16[832,256]{1,0:T(8,128)(2,1)S(1)} fusion(f32[256,256]{1,0:T(8,128)S(1)} %shard_map.49, f32[832,256]{1,0:T(8,128)} %collective-permute-done.13, f32[832,256]{1,0:T(8,128)} %collective-permute-done.11, f32[832,256]{1,0:T(8,128)} %collective-permute-done.12, f32[3328,256]{1,0:T(8,128)S(1)} %shard_map.50, s32[]{:T(128)S(6)} %select_n.99), kind=kOutput, calls=%fused_computation.12 | convolution fusion | flops 655163392 | bytes 4096004 | tf_op jit(solution)/shard_map/dot_general | solution.py:187
  139.7 16.8 %all_to_all.37 = bf16[8,104,256]{2,1,0:T(8,128)(2,1)S(1)} all-to-all(bf16[8,104,256]{2,1,0:T(8,128)(2,1)S(1)} %bitcast.20), channel_id=1, replica_groups=mesh['z'=8,'y'=4,'c'=2,'x'=4] {'z'}, dimensions={0} | all-to-all | bytes 851968 | tf_op jit(solution)/shard_map/all_to_all | solution.py:132
  156.6 15.2 %all_to_all.38 = bf16[8,104,256]{2,1,0:T(8,128)(2,1)S(1)} all-to-all(bf16[8,104,256]{2,1,0:T(8,128)(2,1)S(1)} %broadcast_in_dim.20), channel_id=1, replica_groups=mesh['z'=8,'y'=4,'c'=2,'x'=4] {'z'}, dimensions={0} | all-to-all | bytes 851968 | tf_op jit(solution)/shard_map/all_to_all | solution.py:127
  171.9 20.9 %all_to_all.39 = bf16[4,832,256]{2,1,0:T(8,128)(2,1)S(1)} all-to-all(bf16[4,832,256]{2,1,0:T(8,128)(2,1)S(1)} %broadcast_in_dim.22), channel_id=1, replica_groups=mesh['z'=8,'y'=4,'c'=2,'x'=4] {'y'}, dimensions={0} | all-to-all | bytes 3407872 | tf_op jit(solution)/shard_map/all_to_all | solution.py:127
  192.9 4.7 %collective-permute-start.14 = (bf16[3328,256]{1,0:T(8,128)(2,1)S(1)}, bf16[3328,256]{1,0:T(8,128)(2,1)}, u32[]{:S(2)}, u32[]{:S(2)}) collective-permute-start(bf16[3328,256]{1,0:T(8,128)(2,1)S(1)} %bitcast.19), channel_id=1, source_target_pairs={{0,4},{4,0},{1,5},{5,1},{2,6},{6,2},{3,7},{7,3},{8,12},{12,8},{9,1... | collective-permute-start | bytes 5111816 | tf_op jit(solution)/shard_map/ppermute | solution.py:113
  198.2 2.6 %collective-permute-done.15 = f32[1,256]{1,0:T(1,128)S(1)} collective-permute-done((f32[1,256]{1,0:T(1,128)S(1)}, f32[1,256]{1,0:T(1,128)S(1)}, u32[]{:S(2)}, u32[]{:S(2)}) %collective-permute-start.15) | collective-permute-done | bytes 1056 | tf_op jit(solution)/shard_map/ppermute | solution.py:113
  201.1 2.4 %collective-permute-start.18 = (f32[1,256]{1,0:T(1,128)S(1)}, f32[1,256]{1,0:T(1,128)S(1)}, u32[]{:S(2)}, u32[]{:S(2)}) collective-permute-start(f32[1,256]{1,0:T(1,128)S(1)} %add.143), channel_id=1, source_target_pairs={{0,3},{1,0},{2,1},{3,2},{4,7},{5,4},{6,5},{7,6},{8,11},{9,8},{10,9... | collective-permute-start | bytes 3080 | tf_op jit(solution)/shard_map/ppermute | solution.py:117
  204.5 3.0 %collective-permute-done.16 = f32[1,256]{1,0:T(1,128)S(1)} collective-permute-done((f32[1,256]{1,0:T(1,128)S(1)}, f32[1,256]{1,0:T(1,128)S(1)}, u32[]{:S(2)}, u32[]{:S(2)}) %collective-permute-start.16) | collective-permute-done | bytes 1056 | tf_op jit(solution)/shard_map/ppermute | solution.py:117
  207.5 1.8 broadcast_select_fusion.1
  209.4 0.6 copy-done.6
  210.0 7.6 %fusion.1 = bf16[256,6656]{1,0:T(8,128)(2,1)} fusion(bf16[256,6656]{1,0:T(8,128)(2,1)S(1)} %copy-done.6, bf16[3328,256]{1,0:T(8,128)(2,1)S(1)} %get-tuple-element.8, bf16[3328,256]{1,0:T(8,128)(2,1)S(1)} %get-tuple-element.7, f32[256,256]{1,0:T(8,128)S(1)} %fusion.17), kind=kOutput, calls=%fused_computation.3 | convolution fusion | flops 886112256 | bytes 10485760 | tf_op jit(solution)/shard_map/dot_general | solution.py:207
  217.6 2.8 %convolution_convert_fusion = bf16[256,6656]{1,0:T(8,128)(2,1)} fusion(bf16[3328,256]{1,0:T(8,128)(2,1)S(1)} %get-tuple-element.8, bf16[3328,256]{1,0:T(8,128)(2,1)S(1)} %get-tuple-element.7, f32[256,256]{1,0:T(8,128)S(1)} %fusion.17, f32[256]{0:T(256)S(1)} %bitcast.25), kind=kOutput, calls=%fused_computation.2 | convolution fusion | flops 881065984 | bytes 7078912 | tf_op jit(solution)/shard_map/dot_general | solution.py:207
  220.4 1.6 convolution_divide_fusion
  (56 shorter events, 3.4 us)
Async XLA Ops:
  1.6 5.0 %collective-permute-start.1 = (bf16[4,3328]{1,0:T(4,128)(2,1)S(1)}, bf16[4,3328]{1,0:T(4,128)(2,1)S(1)}, u32[]{:S(2)}, u32[]{:S(2)}) collective-permute-start(bf16[4,3328]{1,0:T(4,128)(2,1)S(1)} %constant_dynamic-slice_fusion.6), channel_id=1, source_target_pairs={{0,4},{4,0},{1,5},{5,1},{2,6},{6,2},{3,7},{7,3},{8,12},{12,8},{9,1... | collective-permute-start | bytes 79880 | tf_op jit(solution)/shard_map/ppermute | solution.py:113
  6.5 26.4 %collective-permute-start = (bf16[256,3328]{1,0:T(8,128)(2,1)S(1)}, bf16[256,3328]{1,0:T(8,128)(2,1)}, u32[]{:S(2)}, u32[]{:S(2)}) collective-permute-start(bf16[256,3328]{1,0:T(8,128)(2,1)S(1)} %constant_dynamic-slice_fusion.7), channel_id=1, source_target_pairs={{0,4},{4,0},{1,5},{5,1},{2,6},{6,2},{3,7},{7,3},{8,12},{12,8},{9,1... | collective-permute-start | bytes 5111816 | tf_op jit(solution)/shard_map/ppermute | solution.py:113
  28.7 24.1 %all-to-all-start.1 = ((bf16[4,8,8,3328]{3,2,1,0:T(8,128)(2,1)}), bf16[4,8,8,3328]{3,2,1,0:T(8,128)(2,1)S(1)}, u32[]{:S(2)}, u32[]{:S(2)}) async-start(bf16[4,8,8,3328]{3,2,1,0:T(8,128)(2,1)} %broadcast_in_dim.17), calls=%async_computation.1 | async-start | bytes 3407872 | tf_op jit(solution)/shard_map/all_to_all | solution.py:127
  52.8 1.5 copy-start.2
  55.3 0.8 copy-start.7
  56.1 26.1 %copy-start.3 = (bf16[256,3328]{1,0:T(8,128)(2,1)S(1)}, bf16[256,3328]{1,0:T(8,128)(2,1)}, u32[]{:S(2)}) copy-start(bf16[256,3328]{1,0:T(8,128)(2,1)} %get-tuple-element.6) | copy-start | bytes 5111812
  56.8 4.7 %collective-permute-start.2 = (f32[256,256]{1,0:T(8,128)}, f32[256,256]{1,0:T(8,128)}, u32[]{:S(2)}, u32[]{:S(2)}) collective-permute-start(f32[256,256]{1,0:T(8,128)} %constant_dynamic-slice_fusion.5), channel_id=1, source_target_pairs={{0,4},{4,0},{1,5},{5,1},{2,6},{6,2},{3,7},{7,3},{8,12},{12,8},{9,1... | collective-permute-start | bytes 786440 | tf_op jit(solution)/shard_map/ppermute | solution.py:113
  63.2 9.0 %collective-permute-start.4 = (f32[256,256]{1,0:T(8,128)}, f32[256,256]{1,0:T(8,128)}, u32[]{:S(2)}, u32[]{:S(2)}) collective-permute-start(f32[256,256]{1,0:T(8,128)} %dynamic-slice_add_fusion), channel_id=1, source_target_pairs={{0,1},{1,2},{2,3},{3,0},{4,5},{5,6},{6,7},{7,4},{8,9},{9,10},{10,1... | collective-permute-start | bytes 786440 | tf_op jit(solution)/shard_map/ppermute | solution.py:117
  64.4 7.8 %collective-permute-start.5 = (f32[256,256]{1,0:T(8,128)}, f32[256,256]{1,0:T(8,128)}, u32[]{:S(2)}, u32[]{:S(2)}) collective-permute-start(f32[256,256]{1,0:T(8,128)} %dynamic-slice_add_fusion), channel_id=1, source_target_pairs={{0,3},{1,0},{2,1},{3,2},{4,7},{5,4},{6,5},{7,6},{8,11},{9,8},{10,9... | collective-permute-start | bytes 786440 | tf_op jit(solution)/shard_map/ppermute | solution.py:117
  65.9 13.0 %collective-permute-start.3 = (f32[256,256]{1,0:T(8,128)}, f32[256,256]{1,0:T(8,128)}, u32[]{:S(2)}, u32[]{:S(2)}) collective-permute-start(f32[256,256]{1,0:T(8,128)} %dynamic-slice_add_fusion), channel_id=1, source_target_pairs={{0,2},{1,3},{2,0},{3,1},{4,6},{5,7},{6,4},{7,5},{8,10},{9,11},{10,... | collective-permute-start | bytes 786440 | tf_op jit(solution)/shard_map/ppermute | solution.py:117
  80.1 5.8 %copy-start.4 = (f32[256,256]{1,0:T(8,128)}, f32[256,256]{1,0:T(8,128)S(1)}, u32[]{:S(2)}) copy-start(f32[256,256]{1,0:T(8,128)S(1)} %add_add_fusion) | copy-start | bytes 786436
  80.7 5.2 %collective-permute-start.10 = (f32[256,256]{1,0:T(8,128)S(1)}, f32[256,256]{1,0:T(8,128)S(1)}, u32[]{:S(2)}, u32[]{:S(2)}) collective-permute-start(f32[256,256]{1,0:T(8,128)S(1)} %add_add_fusion), channel_id=1, source_target_pairs={{0,4},{4,0},{1,5},{5,1},{2,6},{6,2},{3,7},{7,3},{8,12},{12,8},{9,1... | collective-permute-start | bytes 786440 | tf_op jit(solution)/shard_map/ppermute | solution.py:113
  82.0 1.2 collective-permute-start.6
  83.3 11.7 %collective-permute-start.8 = (f32[32,256]{1,0:T(8,128)S(1)}, f32[32,256]{1,0:T(8,128)S(1)}, u32[]{:S(2)}, u32[]{:S(2)}) collective-permute-start(f32[32,256]{1,0:T(8,128)S(1)} %dynamic-slice_add_fusion.1), channel_id=1, source_target_pairs={{0,8},{8,16},{16,24},{24,0},{1,9},{9,17},{17,25},{25,1},{2,10},{10... | collective-permute-start | bytes 98312 | tf_op jit(solution)/shard_map/ppermute | solution.py:117
  83.5 14.3 %collective-permute-start.9 = (f32[32,256]{1,0:T(8,128)S(1)}, f32[32,256]{1,0:T(8,128)S(1)}, u32[]{:S(2)}, u32[]{:S(2)}) collective-permute-start(f32[32,256]{1,0:T(8,128)S(1)} %dynamic-slice_add_fusion.1), channel_id=1, source_target_pairs={{0,24},{8,0},{16,8},{24,16},{1,25},{9,1},{17,9},{25,17},{2,26},{10... | collective-permute-start | bytes 98312 | tf_op jit(solution)/shard_map/ppermute | solution.py:117
  85.9 12.0 %collective-permute-start.7 = (f32[32,256]{1,0:T(8,128)S(1)}, f32[32,256]{1,0:T(8,128)S(1)}, u32[]{:S(2)}, u32[]{:S(2)}) collective-permute-start(f32[32,256]{1,0:T(8,128)S(1)} %dynamic-slice_add_fusion.1), channel_id=1, source_target_pairs={{0,16},{8,24},{16,0},{24,8},{1,17},{9,25},{17,1},{25,9},{2,18},{10... | collective-permute-start | bytes 98312 | tf_op jit(solution)/shard_map/ppermute | solution.py:117
  93.5 43.6 %collective-permute-start.13 = (f32[832,256]{1,0:T(8,128)}, f32[832,256]{1,0:T(8,128)}, u32[]{:S(2)}, u32[]{:S(2)}) collective-permute-start(f32[832,256]{1,0:T(8,128)} %get-tuple-element.10), channel_id=1, source_target_pairs={{0,24},{8,0},{16,8},{24,16},{1,25},{9,1},{17,9},{25,17},{2,26},{10... | collective-permute-start | bytes 2555912 | tf_op jit(solution)/shard_map/ppermute | solution.py:117
  94.9 42.1 %collective-permute-start.11 = (f32[832,256]{1,0:T(8,128)}, f32[832,256]{1,0:T(8,128)}, u32[]{:S(2)}, u32[]{:S(2)}) collective-permute-start(f32[832,256]{1,0:T(8,128)} %get-tuple-element.11), channel_id=1, source_target_pairs={{0,8},{8,16},{16,24},{24,0},{1,9},{9,17},{17,25},{25,1},{2,10},{10... | collective-permute-start | bytes 2555912 | tf_op jit(solution)/shard_map/ppermute | solution.py:117
  94.9 42.1 %collective-permute-start.12 = (f32[832,256]{1,0:T(8,128)}, f32[832,256]{1,0:T(8,128)}, u32[]{:S(2)}, u32[]{:S(2)}) collective-permute-start(f32[832,256]{1,0:T(8,128)} %get-tuple-element.9), channel_id=1, source_target_pairs={{0,16},{8,24},{16,0},{24,8},{1,17},{9,25},{17,1},{25,9},{2,18},{10... | collective-permute-start | bytes 2555912 | tf_op jit(solution)/shard_map/ppermute | solution.py:117
  111.9 14.5 %all-to-all-start.3 = ((f32[8,32,256]{2,1,0:T(8,128)}), f32[8,32,256]{2,1,0:T(8,128)}, u32[]{:S(2)}, u32[]{:S(2)}) async-start(f32[8,32,256]{2,1,0:T(8,128)} %broadcast_in_dim.19), calls=%async_computation.3 | async-start | bytes 524288 | tf_op jit(solution)/shard_map/all_to_all | solution.py:127
  137.0 2.7 %copy-start = (f32[256,256]{1,0:T(8,128)}, f32[256,256]{1,0:T(8,128)S(1)}, u32[]{:S(2)}) copy-start(f32[256,256]{1,0:T(8,128)S(1)} %shard_map.49) | copy-start | bytes 786436
  171.8 31.7 %copy-start.1 = (f32[256,256]{1,0:T(8,128)S(1)}, f32[256,256]{1,0:T(8,128)}, u32[]{:S(2)}) copy-start(f32[256,256]{1,0:T(8,128)} %copy-done) | copy-start | bytes 786436
  171.8 31.7 %copy-start.5 = (f32[256,256]{1,0:T(8,128)S(1)}, f32[256,256]{1,0:T(8,128)}, u32[]{:S(2)}) copy-start(f32[256,256]{1,0:T(8,128)} %copy-done.4) | copy-start | bytes 786436
  192.9 14.7 %collective-permute-start.14 = (bf16[3328,256]{1,0:T(8,128)(2,1)S(1)}, bf16[3328,256]{1,0:T(8,128)(2,1)}, u32[]{:S(2)}, u32[]{:S(2)}) collective-permute-start(bf16[3328,256]{1,0:T(8,128)(2,1)S(1)} %bitcast.19), channel_id=1, source_target_pairs={{0,4},{4,0},{1,5},{5,1},{2,6},{6,2},{3,7},{7,3},{8,12},{12,8},{9,1... | collective-permute-start | bytes 5111816 | tf_op jit(solution)/shard_map/ppermute | solution.py:113
  198.1 2.8 %collective-permute-start.15 = (f32[1,256]{1,0:T(1,128)S(1)}, f32[1,256]{1,0:T(1,128)S(1)}, u32[]{:S(2)}, u32[]{:S(2)}) collective-permute-start(f32[1,256]{1,0:T(1,128)S(1)} %bitcast.23), channel_id=1, source_target_pairs={{0,4},{4,0},{1,5},{5,1},{2,6},{6,2},{3,7},{7,3},{8,12},{12,8},{9,1... | collective-permute-start | bytes 3080 | tf_op jit(solution)/shard_map/ppermute | solution.py:113
  200.8 3.6 %collective-permute-start.17 = (f32[1,256]{1,0:T(1,128)S(1)}, f32[1,256]{1,0:T(1,128)S(1)}, u32[]{:S(2)}, u32[]{:S(2)}) collective-permute-start(f32[1,256]{1,0:T(1,128)S(1)} %add.143), channel_id=1, source_target_pairs={{0,1},{1,2},{2,3},{3,0},{4,5},{5,6},{6,7},{7,4},{8,9},{9,10},{10,1... | collective-permute-start | bytes 3080 | tf_op jit(solution)/shard_map/ppermute | solution.py:117
  201.1 3.3 %collective-permute-start.18 = (f32[1,256]{1,0:T(1,128)S(1)}, f32[1,256]{1,0:T(1,128)S(1)}, u32[]{:S(2)}, u32[]{:S(2)}) collective-permute-start(f32[1,256]{1,0:T(1,128)S(1)} %add.143), channel_id=1, source_target_pairs={{0,3},{1,0},{2,1},{3,2},{4,7},{5,4},{6,5},{7,6},{8,11},{9,8},{10,9... | collective-permute-start | bytes 3080 | tf_op jit(solution)/shard_map/ppermute | solution.py:117
  203.5 3.9 %collective-permute-start.16 = (f32[1,256]{1,0:T(1,128)S(1)}, f32[1,256]{1,0:T(1,128)S(1)}, u32[]{:S(2)}, u32[]{:S(2)}) collective-permute-start(f32[1,256]{1,0:T(1,128)S(1)} %add.143), channel_id=1, source_target_pairs={{0,2},{1,3},{2,0},{3,1},{4,6},{5,7},{6,4},{7,5},{8,10},{9,11},{10,... | collective-permute-start | bytes 3080 | tf_op jit(solution)/shard_map/ppermute | solution.py:117
  207.5 2.5 %copy-start.6 = (bf16[256,6656]{1,0:T(8,128)(2,1)S(1)}, bf16[256,6656]{1,0:T(8,128)(2,1)}, u32[]{:S(2)}) copy-start(bf16[256,6656]{1,0:T(8,128)(2,1)} %param.2) | copy-start | bytes 10223620
